TPU v7x, 512 devices: a whole 4x4x16 slice. The times are simulated.
512 devices in a mesh: seq: 64 (over z, y), mp: 8 (over x, core).
Axes of the slice: x: 4, y: 4, z: 16, core: 2. Of those that a mesh axis runs over, the one named last changes fastest.
Arguments:
- shared_qk: bfloat16 [8192, 4096], P('seq', 'mp'), may hold values from -40 to 40
- values: bfloat16 [8192, 4096], P('seq', 'mp'), may hold values from -6 to 6
- buckets: int32 [8192, 32], P('seq', 'mp'), may hold values from 0 to 63, as said below
- counts: int32 [64, 32, 64], P(None, 'mp'), may hold values from 0 to 4, as said below
- w_out: bfloat16 [4096, 4096], P('mp'), may hold values from -0.09375 to 0.09375
Outputs:
- projected: bfloat16 [8192, 4096], P('seq', 'mp')
Inputs may be any that keep to these rules, and one draw needn't show every extreme that they name: `buckets`: in each head at most 4 tokens among rows d * 128 to (d + 1) * 128 - 1 name one bucket, and in each head one bucket is named by exactly 4 tokens of every such group of rows. counts[d, h, b] is the number of rows among d * 128 to (d + 1) * 128 - 1 whose bucket in head h is b.
All inputs are finite; a program needn't handle non-finite values.
Results may differ from a plain program's by a relative error of at most 0.0057.
Values may be sent and summed in bfloat16 or wider, within the bound.
A program may use at most 64 MiB of HBM per device.

v0:
```python
import math

import jax
import jax.numpy as jnp
from jax import lax
from jax.sharding import PartitionSpec as P

BLOCK = 256


SELF_SCORE = -100000.0


def passed_along(shard, axis, by):
    devices = lax.axis_size(axis)
    return lax.ppermute(shard, axis, [(i, (i + by) % devices) for i in range(devices)])


def block_attention(queries, window, window_live):
    head_dim = queries.shape[-1]
    block_rows = queries.shape[-2]
    key_rows = window[..., :head_dim]
    value_rows = window[..., head_dim:]
    scores = jnp.einsum("cqd,ckd->cqk", queries, key_rows, preferred_element_type=jnp.float32) * (
        1.0 / math.sqrt(head_dim)
    )
    query_place = jnp.arange(block_rows)[:, None] + block_rows
    key_place = jnp.arange(2 * block_rows)[None, :]
    itself = query_place == key_place
    scores = jnp.where(itself[None], SELF_SCORE, scores)
    allowed = window_live[:, None, :] | itself[None]
    row_max = jnp.max(jnp.where(allowed, scores, -1e30), axis=-1, keepdims=True)
    exp_terms = jnp.where(allowed, jnp.exp(scores - row_max), 0.0)
    weights = (exp_terms / jnp.sum(exp_terms, axis=-1, keepdims=True)).astype(jnp.bfloat16)
    attended = jnp.einsum("cqk,ckd->cqd", weights, value_rows, preferred_element_type=jnp.float32)
    return attended.astype(jnp.bfloat16)


def owner_layout(received, column, slot_count):
    source_count = column.shape[0]
    head_count = column.shape[1]
    upto_count = jnp.cumsum(column, axis=0)
    before_count = upto_count - column
    bucket_total = upto_count[-1]
    slot_range = jnp.arange(slot_count)
    source_dev = jnp.sum(upto_count[:, :, None] <= slot_range[None, None, :], axis=0)
    source_dev = jnp.minimum(source_dev, source_count - 1)
    source_range = jnp.arange(source_count)
    source_start = jnp.sum(
        jnp.where(source_dev[None] == source_range[:, None, None], before_count[:, :, None], 0),
        axis=0,
    )
    entry_row = jnp.clip(slot_range[None, :] - source_start, 0, received.shape[2] - 1)
    head_range = jnp.arange(head_count)
    layout = received[source_dev, head_range[:, None], entry_row]
    live = slot_range[None, :] < bucket_total[:, None]
    layout = jnp.where(live[..., None], layout, jnp.zeros((), layout.dtype))
    return (layout, live, before_count, bucket_total)


def tail_live(bucket_total, block_rows):
    return bucket_total[:, None] - block_rows + jnp.arange(block_rows)[None, :] >= 0


def last_rows(layout, bucket_total, block_rows):
    rank_index = bucket_total[:, None] - block_rows + jnp.arange(block_rows)[None, :]
    head_range = jnp.arange(layout.shape[0])
    rows = layout[head_range[:, None], jnp.maximum(rank_index, 0)]
    return jnp.where((rank_index >= 0)[..., None], rows, jnp.zeros((), rows.dtype))


def local(shared_qk, values, buckets, counts, w_out):
    tok_rows = shared_qk.shape[0]
    head_count = buckets.shape[1]
    head_dim = shared_qk.shape[1] // head_count
    seq_count = lax.axis_size("seq")
    capacity = 2 * tok_rows // seq_count
    slot_count = seq_count * capacity
    block_rows = BLOCK
    block_count = slot_count // block_rows
    own_index = lax.axis_index("seq")
    prev_index = (own_index + seq_count - 1) % seq_count
    head_range = jnp.arange(head_count)
    bucket_heads = buckets.T
    positions = jnp.arange(tok_rows)
    earlier = positions[None, :] < positions[:, None]
    same_bucket = bucket_heads[:, :, None] == bucket_heads[:, None, :]
    within = jnp.sum(same_bucket & earlier[None], axis=2)
    own_counts = lax.dynamic_index_in_dim(counts, own_index, 0, keepdims=False)
    own_starts = jnp.cumsum(own_counts, axis=1) - own_counts
    bucket_range = jnp.arange(seq_count)
    one_hot = bucket_heads[:, :, None] == bucket_range[None, None, :]
    token_start = jnp.sum(jnp.where(one_hot, own_starts[:, None, :], 0), axis=2)
    sorted_pos = token_start + within
    token_order = jnp.sum(
        jnp.where(sorted_pos[:, :, None] == positions[None, None, :], positions[None, :, None], 0),
        axis=1,
    )
    slot_range = jnp.arange(capacity)
    send_index = own_starts.T[:, :, None] + slot_range[None, None, :]
    filled = slot_range[None, None, :] < own_counts.T[:, :, None]
    token_pick = token_order[head_range[None, :, None], jnp.minimum(send_index, tok_rows - 1)]
    packed = jnp.concatenate(
        [
            shared_qk.reshape(tok_rows, head_count, head_dim),
            values.reshape(tok_rows, head_count, head_dim),
        ],
        axis=2,
    )
    outgoing = packed[token_pick, head_range[None, :, None]]
    outgoing = jnp.where(filled[..., None], outgoing, jnp.zeros((), outgoing.dtype))
    own_column = lax.dynamic_index_in_dim(counts, own_index, 2, keepdims=False)
    prev_column = lax.dynamic_index_in_dim(counts, prev_index, 2, keepdims=False)
    prev_total = jnp.sum(prev_column, axis=0)
    received = lax.all_to_all(outgoing, "seq", split_axis=0, concat_axis=0, tiled=True)
    layout, live, before_count, bucket_total = owner_layout(received, own_column, slot_count)
    tail_rows = last_rows(layout, bucket_total, block_rows)
    prev_rows = passed_along(tail_rows, "seq", 1)
    prev_live = tail_live(prev_total, block_rows)
    keys_all = jnp.concatenate([prev_rows, layout], axis=1)
    live_all = jnp.concatenate([prev_live, live], axis=1)
    window = jnp.concatenate(
        [
            keys_all[:, :slot_count].reshape(head_count, block_count, block_rows, 2 * head_dim),
            keys_all[:, block_rows:].reshape(head_count, block_count, block_rows, 2 * head_dim),
        ],
        axis=2,
    )
    window_live = jnp.concatenate(
        [
            live_all[:, :slot_count].reshape(head_count, block_count, block_rows),
            live_all[:, block_rows:].reshape(head_count, block_count, block_rows),
        ],
        axis=2,
    )
    queries = layout[..., :head_dim].reshape(head_count, block_count, block_rows, head_dim)
    attended = lax.map(
        lambda per_head: block_attention(per_head[0], per_head[1], per_head[2]),
        (queries, window, window_live),
    )
    out_layout = attended.reshape(head_count, slot_count, head_dim)
    back_index = before_count[:, :, None] + slot_range[None, None, :]
    back_filled = slot_range[None, None, :] < own_column[:, :, None]
    back_rows = out_layout[head_range[None, :, None], jnp.minimum(back_index, slot_count - 1)]
    back_rows = jnp.where(back_filled[..., None], back_rows, jnp.zeros((), back_rows.dtype))
    returned = lax.all_to_all(back_rows, "seq", split_axis=0, concat_axis=0, tiled=True)
    token_out = returned[buckets, head_range[None, :], within.T]
    token_out = token_out.reshape(tok_rows, head_count * head_dim)
    partial_sum = jnp.dot(token_out, w_out, preferred_element_type=jnp.float32)
    projected = lax.psum_scatter(partial_sum, "mp", scatter_dimension=1, tiled=True)
    return projected.astype(jnp.bfloat16)


def solution(mesh):
    placed = (P("seq", "mp"), P("seq", "mp"), P("seq", "mp"), P(None, "mp", None), P("mp", None))
    return jax.shard_map(
        local, mesh=mesh, in_specs=placed, out_specs=P("seq", "mp"), check_vma=False
    )
```

profile of v0, /device:TPU:1, one launch (start us, length us, event | category | flops | bytes accessed | tf_op | source)
XLA Modules:
  0.0 193.1 jit_solution(6731412304890291498)
XLA Ops:
  6.6 0.7 dynamic-slice_bitcast_fusion.1
  7.2 0.2 reduce_window_sum.25
  7.5 0.8 select_reduce_fusion.3
  8.3 1.0 convert_reduce_fusion.1
  9.3 0.2 select_reduce_fusion.2
  9.5 0.1 copy.25
  9.6 0.1 iota_compare_fusion.5
  9.7 0.1 copy.26
  9.8 0.2 fusion.12
  10.0 0.2 reshape.373
  10.1 8.8 %gather_fusion = s32[1024]{0:T(1024)S(1)} fusion(s32[4,128]{1,0:T(4,128)S(1)} %select_reduce_fusion.2, s32[1024]{0:T(1024)S(1)} %reshape.373), kind=kCustom, calls=%fused_computation | custom fusion | bytes 16384 | tf_op jit(solution)/shard_map/gather | solution.py:102
  18.9 0.2 gather.23
  19.1 0.1 fusion.15
  19.2 0.2 reshape.379
  19.4 0.1 pad_maximum_fusion
  19.6 5.8 %gather_fusion.1 = bf16[1024,256]{1,0:T(8,128)(2,1)S(1)} fusion(bf16[128,4,256]{2,1,0:T(4,128)(2,1)S(1)} %pad_maximum_fusion, s32[1024]{0:T(1024)S(1)} %reshape.379), kind=kCustom, calls=%fused_computation.1 | custom fusion | bytes 1056768 | tf_op jit(solution)/shard_map/gather | solution.py:110
  25.4 0.1 reshape.382
  25.5 1.2 broadcast_select_fusion.2
  26.7 19.3 %all-to-all-start = ((bf16[64,4,4,256]{3,2,1,0:T(4,128)(2,1)}), bf16[64,4,4,256]{3,2,1,0:T(4,128)(2,1)S(1)}, u32[]{:S(2)}, u32[]{:S(2)}) async-start(bf16[64,4,4,256]{3,2,1,0:T(4,128)(2,1)} %broadcast_select_fusion.2), calls=%async_computation | async-start | bytes 1048576 | tf_op jit(solution)/shard_map/all_to_all | solution.py:115
  46.0 0.3 dynamic-slice_reduce_fusion
  46.3 0.5 copy.34
  46.8 0.1 reduce_window_sum.24
  47.0 0.1 convert_reduce_fusion
  47.2 0.1 or_bitcast_fusion
  47.3 0.1 select_reduce_fusion.1
  47.5 0.1 add_compare_fusion
  47.5 0.1 iota_compare_fusion.8
  47.6 0.1 iota_compare_fusion.9
  47.7 0.1 iota_compare_fusion.6
  47.8 0.2 fusion.18
  48.0 28.0 %all-to-all-done = bf16[64,4,4,256]{3,2,1,0:T(4,128)(2,1)S(1)} async-done(((bf16[64,4,4,256]{3,2,1,0:T(4,128)(2,1)}), bf16[64,4,4,256]{3,2,1,0:T(4,128)(2,1)S(1)}, u32[]{:S(2)}, u32[]{:S(2)}) %all-to-all-start) | async-done | bytes 524320 | tf_op jit(solution)/shard_map/all_to_all | solution.py:115
  76.0 6.9 %gather_fusion.2 = bf16[1024,256]{1,0:T(8,128)(2,1)S(1)} fusion(bf16[64,4,4,256]{3,2,1,0:T(4,128)(2,1)S(1)} %all-to-all-done, s32[1024]{0:T(1024)S(1)} %bitcast.102), kind=kCustom, calls=%fused_computation.2 | custom fusion | bytes 1060864 | tf_op jit(solution)/shard_map/gather | solution.py:55
  83.0 0.2 broadcast_select_fusion.3
  83.2 5.8 %gather_fusion.3 = bf16[1024,256]{1,0:T(8,128)(2,1)S(1)} fusion(bf16[4,256,256]{2,1,0:T(8,128)(2,1)S(1)} %broadcast_select_fusion.3, s32[1024]{0:T(1024)S(1)} %bitcast.101), kind=kCustom, calls=%fused_computation.3 | custom fusion | bytes 1056768 | tf_op jit(solution)/shard_map/gather | solution.py:68
  89.0 0.2 broadcast_select_fusion.1
  89.2 3.4 %collective-permute-start = (bf16[4,256,256]{2,1,0:T(8,128)(2,1)S(1)}, bf16[4,256,256]{2,1,0:T(8,128)(2,1)S(1)}, u32[]{:S(2)}, u32[]{:S(2)}) collective-permute-start(bf16[4,256,256]{2,1,0:T(8,128)(2,1)S(1)} %broadcast_select_fusion.1), channel_id=1, source_target_pairs={{0,8},{8,16},{16,24},{24,32},{32,40},{40,48},{48,56},{56,64},{64,7... | collective-permute-start | bytes 1572872 | tf_op jit(solution)/shard_map/ppermute | solution.py:16
  92.6 0.2 reshape.397
  92.8 0.2 broadcast_select_fusion
  93.0 11.1 %collective-permute-done = bf16[4,256,256]{2,1,0:T(8,128)(2,1)S(1)} collective-permute-done((bf16[4,256,256]{2,1,0:T(8,128)(2,1)S(1)}, bf16[4,256,256]{2,1,0:T(8,128)(2,1)S(1)}, u32[]{:S(2)}, u32[]{:S(2)}) %collective-permute-start) | collective-permute-done | bytes 524320 | tf_op jit(solution)/shard_map/ppermute | solution.py:16
  104.2 4.7 %while.10 = (s32[]{:T(128)}, bf16[4,1,256,128]{3,2,1,0:T(8,128)(2,1)S(1)}, pred[4,1,512]{2,0,1:T(4,128)(4,1)S(1)}, bf16[4,1,256,128]{3,2,1,0:T(8,128)(2,1)S(1)}, bf16[4,1,512,256]{3,2,1,0:T(8,128)(2,1)S(1)}, /*index=5*/s32[]{:T(128)}) while((s32[]{:T(128)}, bf16[4,1,256,128]{3,2,1,0:T(8,128)(2,1)S(1)}, pred[4,1,512]{2,0,1:T(4,128)(4,1)S(1)}, ...), condition=%wide.region_11.12_spmd, body=%wide.region_8.11_spmd.sunk | while | flops 69369600 | bytes 2502237 | solution.py:137
  104.2 0.4 select_reduce_fusion.5
  104.6 0.3 fusion.42
  104.9 0.4 fusion.43
  105.4 0.4 select_reduce_fusion.5
  105.8 0.3 fusion.42
  106.1 0.4 fusion.43
  106.6 0.4 select_reduce_fusion.5
  106.9 0.3 fusion.42
  107.3 0.4 fusion.43
  107.7 0.4 select_reduce_fusion.5
  108.1 0.3 fusion.42
  108.4 0.4 fusion.43
  108.9 5.8 %gather_fusion.4 = bf16[1024,128]{1,0:T(8,128)(2,1)S(1)} fusion(bf16[4,256,128]{2,1,0:T(8,128)(2,1)S(1)} %bitcast.103, s32[1024]{0:T(1024)S(1)} %reshape.397), kind=kCustom, calls=%fused_computation.4 | custom fusion | bytes 532480 | tf_op jit(solution)/shard_map/gather | solution.py:144
  114.7 1.0 broadcast_select_fusion.4
  115.7 7.7 %all-to-all-start.1 = ((bf16[64,4,4,128]{3,2,1,0:T(4,128)(2,1)}), bf16[64,4,4,128]{3,2,1,0:T(4,128)(2,1)S(1)}, u32[]{:S(2)}, u32[]{:S(2)}) async-start(bf16[64,4,4,128]{3,2,1,0:T(4,128)(2,1)} %broadcast_select_fusion.4), calls=%async_computation.1 | async-start | bytes 524288 | tf_op jit(solution)/shard_map/all_to_all | solution.py:146
  123.4 0.2 reduce-scatter.2.cloned.1.call-start
  123.7 0.1 copy.32
  123.8 0.1 reshape.403
  123.9 17.2 %all-to-all-done.1 = bf16[64,4,4,128]{3,2,1,0:T(4,128)(2,1)S(1)} async-done(((bf16[64,4,4,128]{3,2,1,0:T(4,128)(2,1)}), bf16[64,4,4,128]{3,2,1,0:T(4,128)(2,1)S(1)}, u32[]{:S(2)}, u32[]{:S(2)}) %all-to-all-start.1) | async-done | bytes 262176 | tf_op jit(solution)/shard_map/all_to_all | solution.py:146
  141.1 3.7 %gather_fusion.5 = bf16[512,128]{1,0:T(8,128)(2,1)S(1)} fusion(bf16[64,4,4,128]{3,2,1,0:T(4,128)(2,1)S(1)} %all-to-all-done.1, s32[512]{0:T(512)S(1)} %reshape.403), kind=kCustom, calls=%fused_computation.5 | custom fusion | bytes 268288 | tf_op jit(solution)/shard_map/gather | solution.py:147
  144.8 0.1 reshape.372
  144.9 4.3 %fusion.37 = f32[128,4096]{1,0:T(8,128)} fusion(bf16[128,512]{1,0:T(8,128)(2,1)S(1)} %reshape.372, bf16[512,4096]{1,0:T(8,128)(2,1)} %param.11), kind=kOutput, calls=%fused_computation.99 | convolution fusion | flops 536870912 | bytes 6422528 | tf_op jit(solution)/shard_map/dot_general | solution.py:149
  149.2 35.4 %reduce-scatter.2.cloned.1.call-done = f32[128,512]{1,0:T(8,128)} async-done(((f32[128,4096]{1,0:T(8,128)}), f32[128,512]{1,0:T(8,128)}) %reduce-scatter.2.cloned.1.call-update) | async-done | bytes 262160 | tf_op jit(solution)/shard_map/reduce_scatter | solution.py:150
  184.6 1.6 convert_element_type.19
  (41 shorter events, 0.7 us)
Async XLA Ops:
  10.1 9.2 %copy-start.1 = (bf16[128,512]{1,0:T(8,128)(2,1)S(1)}, bf16[128,512]{1,0:T(8,128)(2,1)}, u32[]{:S(2)}) copy-start(bf16[128,512]{1,0:T(8,128)(2,1)} %param.7) | copy-start | bytes 393220
  10.1 9.3 %copy-start.2 = (bf16[128,512]{1,0:T(8,128)(2,1)S(1)}, bf16[128,512]{1,0:T(8,128)(2,1)}, u32[]{:S(2)}) copy-start(bf16[128,512]{1,0:T(8,128)(2,1)} %param.8) | copy-start | bytes 393220
  25.4 20.6 %copy-start = (s32[64,4,64]{2,1,0:T(4,128)S(1)}, s32[64,4,64]{2,1,0:T(4,128)}, u32[]{:S(2)}) copy-start(s32[64,4,64]{2,1,0:T(4,128)} %param.10) | copy-start | bytes 196612
  26.7 49.3 %all-to-all-start = ((bf16[64,4,4,256]{3,2,1,0:T(4,128)(2,1)}), bf16[64,4,4,256]{3,2,1,0:T(4,128)(2,1)S(1)}, u32[]{:S(2)}, u32[]{:S(2)}) async-start(bf16[64,4,4,256]{3,2,1,0:T(4,128)(2,1)} %broadcast_select_fusion.2), calls=%async_computation | async-start | bytes 1048576 | tf_op jit(solution)/shard_map/all_to_all | solution.py:115
  89.2 14.9 %collective-permute-start = (bf16[4,256,256]{2,1,0:T(8,128)(2,1)S(1)}, bf16[4,256,256]{2,1,0:T(8,128)(2,1)S(1)}, u32[]{:S(2)}, u32[]{:S(2)}) collective-permute-start(bf16[4,256,256]{2,1,0:T(8,128)(2,1)S(1)} %broadcast_select_fusion.1), channel_id=1, source_target_pairs={{0,8},{8,16},{16,24},{24,32},{32,40},{40,48},{48,56},{56,64},{64,7... | collective-permute-start | bytes 1572872 | tf_op jit(solution)/shard_map/ppermute | solution.py:16
  108.8 14.8 %copy-start.3 = (s32[128,4]{0,1:T(4,128)S(1)}, s32[128,4]{0,1:T(4,128)}, u32[]{:S(2)}) copy-start(s32[128,4]{0,1:T(4,128)} %param.9) | copy-start | bytes 6148
  115.7 25.4 %all-to-all-start.1 = ((bf16[64,4,4,128]{3,2,1,0:T(4,128)(2,1)}), bf16[64,4,4,128]{3,2,1,0:T(4,128)(2,1)S(1)}, u32[]{:S(2)}, u32[]{:S(2)}) async-start(bf16[64,4,4,128]{3,2,1,0:T(4,128)(2,1)} %broadcast_select_fusion.4), calls=%async_computation.1 | async-start | bytes 524288 | tf_op jit(solution)/shard_map/all_to_all | solution.py:146
  123.4 61.2 %reduce-scatter.2.cloned.1.call-start = ((), (), s32[]{:S(2)}) async-start(), calls=%async_computation.3 | async-start | bytes 2359296 | tf_op jit(solution)/shard_map/reduce_scatter | solution.py:150
Sparse Core Ops, SparseCore 0:
  149.3 35.2 reduce-scatter.1
where the time goes:
time: 194 us; the launch traced here: 193 us
  waiting for transfers between devices  91.7 us (47%)
  local copies, waits for them, and re-layouts  39.8 us (21%)
  starting transfers between devices  30.6 us (16%)
  between operations  13.7 us (7%)
  other arithmetic  9.82 us (5%)
  matrix products  7.33 us (4%)
    reduce_scatter x1, waiting for transfers between devices, local(): lax.psum_scatter(partial_sum, 'mp', scatter_dimension=1, tiled=True)  35.4 us
    all_to_all x1, waiting for transfers between devices, local(): lax.all_to_all(outgoing, 'seq', split_axis=0, concat_axis=0, tiled=True)  28 us
    all_to_all x1, starting transfers between devices, local(): lax.all_to_all(outgoing, 'seq', split_axis=0, concat_axis=0, tiled=True)  19.3 us
    all_to_all x1, waiting for transfers between devices, local(): lax.all_to_all(back_rows, 'seq', split_axis=0, concat_axis=0, tiled=True)  17.2 us
    ppermute x1, waiting for transfers between devices, passed_along(): lax.ppermute(shard, axis, [(i, (i + by) % devices) for i in range(devices)])  11.1 us
    gather x2, local copies, waits for them, and re-layouts, local(): token_order[head_range[None, :, None], jnp.minimum(send_index, tok_rows -...  8.96 us
    all_to_all x1, starting transfers between devices, local(): lax.all_to_all(back_rows, 'seq', split_axis=0, concat_axis=0, tiled=True)  7.72 us
    gather x1, local copies, waits for them, and re-layouts, owner_layout(): layout = received[source_dev, head_range[:, None], entry_row]  6.93 us
  transfers between devices with their start and end apart: 4, of which 4 were waited for; matrix products, arithmetic and copies ran while one was open for 1% of the time, Pallas kernels for 0%

commit v1 on v0

v1 whole, which is shorter than its diff:
```python
import functools
import math

import jax
import jax.numpy as jnp
from jax import lax
from jax.experimental import pallas as pl
from jax.experimental.pallas import tpu as pltpu
from jax.sharding import PartitionSpec as P

CAP = 4
SELF_SCORE = -100000.0
DEAD = -1e30
BF16 = jnp.bfloat16
F32 = jnp.float32
MESH = pl.DeviceIdType.MESH


def iota(shape, dim):
    return lax.broadcasted_iota(jnp.int32, shape, dim)


def one_hot(mask):
    return jnp.where(mask, 1.0, 0.0).astype(BF16)


def dot(a, b):
    return jnp.dot(a, b, preferred_element_type=F32)


def layer_kernel(
    planes, heads, chips, tok, dim,
    qk_ref, val_ref, buckets_ref, counts_ref, w_ref, out_ref,
    w_buf, out_pack, in_pack, rows_buf, prev_buf, att_buf, out_ret, in_ret, tok_buf, pick_buf,
    pair_out, pair_in, chip_out, chip_in,
    w_sem, pack_send, pack_recv, next_send, next_recv, ret_send, ret_recv,
    pair_send, pair_recv, chip_send, chip_recv,
):
    devices = planes * heads
    slots = devices * CAP
    unit = heads * CAP
    groups = devices // 16
    span = 16 * unit
    part = 16 * CAP
    block = w_ref.shape[1] // (2 * chips)
    me = lax.axis_index("seq")
    mp = lax.axis_index("mp")
    z, y = me // heads, lax.rem(me, heads)
    x, core = mp // 2, lax.rem(mp, 2)

    load_w = pltpu.make_async_copy(w_ref, w_buf, w_sem)
    load_w.start()

    barrier = pltpu.get_barrier_semaphore()

    def greet(k, carry):
        other = lax.rem(me + k, devices)
        pl.semaphore_signal(barrier, inc=1, device_id=(other, mp), device_id_type=MESH)
        return carry

    lax.fori_loop(1, devices, greet, 0)
    pl.semaphore_signal(barrier, inc=1, device_id=(me, x * 2 + 1 - core), device_id_type=MESH)
    for off in range(1, chips):
        there = lax.rem(x + off, chips) * 2 + core
        pl.semaphore_signal(barrier, inc=1, device_id=(me, there), device_id_type=MESH)

    eye = iota((tok, tok), 0) == iota((tok, tok), 1)
    before = iota((tok, tok), 0) < iota((tok, tok), 1)
    after = iota((tok, tok), 0) > iota((tok, tok), 1)
    for h in range(heads):
        b_col = buckets_ref[:, h : h + 1]
        b_row = jnp.sum(jnp.where(eye, b_col, 0), axis=0, keepdims=True)
        same = b_col == b_row
        rank_row = jnp.sum(jnp.where(same & before, 1, 0), axis=0, keepdims=True)
        rank_col = jnp.sum(jnp.where(same & after, 1, 0), axis=1, keepdims=True)
        place = one_hot(iota((slots, tok), 0) == b_row * CAP + rank_row)
        pick_buf[h] = one_hot(iota((tok, slots), 1) == b_col * CAP + rank_col)
        cols = slice(h * dim, (h + 1) * dim)
        rows = slice(h * slots, (h + 1) * slots)
        out_pack[rows, :dim] = dot(place, qk_ref[:, cols]).astype(BF16)
        out_pack[rows, dim:] = dot(place, val_ref[:, cols]).astype(BF16)

    pl.semaphore_wait(barrier, devices - 1 + chips)

    def peer(i):
        a = i // heads
        half = planes // 2
        dz = jnp.where(lax.rem(a, 2) == 1, half - (a + 1) // 2, half + a // 2)
        pz = lax.rem(z + dz, planes)
        py = lax.rem(y + heads - 1 - lax.rem(i, heads), heads)
        return pz, py

    def pack_copy(i):
        pz, py = peer(i)
        src = pl.multiple_of(py * slots + pz * unit, unit)
        dst = pl.multiple_of(me * unit, unit)
        return pltpu.make_async_remote_copy(
            src_ref=out_pack.at[pl.ds(src, unit)],
            dst_ref=in_pack.at[pl.ds(dst, unit)],
            send_sem=pack_send,
            recv_sem=pack_recv.at[me // 16],
            device_id=(pz * heads + py, mp),
            device_id_type=MESH,
        )

    def send_pack(i, carry):
        pack_copy(i).start()
        return carry

    lax.fori_loop(0, devices - 1, send_pack, 0)
    own_src = pl.multiple_of(y * slots + z * unit, unit)
    own_dst = pl.multiple_of(me * unit, unit)
    pltpu.make_async_copy(
        out_pack.at[pl.ds(own_src, unit)], in_pack.at[pl.ds(own_dst, unit)], pack_recv.at[me // 16]
    ).start()

    counts = counts_ref[:, y, :]
    spread = (iota((devices, slots), 1) // CAP) == iota((devices, slots), 0)
    rank = lax.rem(iota((1, slots), 1), CAP)
    dead = []
    for j in range(-1, heads):
        b = lax.rem(z * heads + j + devices, devices)
        column = jnp.sum(jnp.where(iota(counts.shape, 1) == b, counts, 0), axis=1, keepdims=True)
        row = jnp.sum(jnp.where(spread, column, 0), axis=0, keepdims=True)
        dead.append(jnp.where(rank < row, 0.0, DEAD))

    def by_bucket(i):
        return (i // CAP) % 16 * unit + i // part * CAP + i % CAP

    order = one_hot(by_bucket(iota((span, span), 0)) == iota((span, span), 1))
    order_back = one_hot(by_bucket(iota((span, span), 1)) == iota((span, span), 0))

    next_z = lax.rem(z + 1, planes)
    for g in range(groups):
        here = in_pack.at[g * span : (g + 1) * span]
        pltpu.make_async_copy(here, here, pack_recv.at[g]).wait()
        arranged = dot(order, here[...]).astype(BF16)
        rows = slice(g * part, (g + 1) * part)
        for j in range(heads):
            rows_buf[j, rows, :] = arranged[j * part : (j + 1) * part]
        pltpu.make_async_remote_copy(
            src_ref=rows_buf.at[heads - 1, rows],
            dst_ref=prev_buf.at[rows],
            send_sem=next_send,
            recv_sem=next_recv,
            device_id=(next_z * heads + y, mp),
            device_id_type=MESH,
        ).start()

    itself = iota((slots, slots), 0) == iota((slots, slots), 1)
    scale = 1.0 / math.sqrt(dim)

    def attend(j, prev):
        q = rows_buf[j, :, :dim]
        v = rows_buf[j, :, dim:]
        trans = (((1,), (1,)), ((), ()))
        own = lax.dot_general(q, q, trans, preferred_element_type=F32)
        own = jnp.where(itself, SELF_SCORE, own * scale + dead[j + 1])
        far = lax.dot_general(q, prev[:, :dim], trans, preferred_element_type=F32) * scale + dead[j]
        top = jnp.maximum(jnp.max(own, axis=1, keepdims=True), jnp.max(far, axis=1, keepdims=True))
        own = jnp.exp(own - top)
        far = jnp.exp(far - top)
        total = jnp.sum(own, axis=1, keepdims=True) + jnp.sum(far, axis=1, keepdims=True)
        share = 1.0 / total
        att = dot((own * share).astype(BF16), v) + dot((far * share).astype(BF16), prev[:, dim:])
        att_buf[j] = att.astype(BF16)

    for j in range(1, heads):
        attend(j, rows_buf[j - 1])
    pltpu.make_async_copy(prev_buf, prev_buf, next_recv).wait()
    attend(0, prev_buf[...])

    for g in range(groups):
        rows = slice(g * part, (g + 1) * part)
        mine = jnp.concatenate([att_buf[j, rows, :] for j in range(heads)], axis=0)
        out_ret[g * span : (g + 1) * span, :] = dot(order_back, mine).astype(BF16)

    def ret_copy(i):
        pz, py = peer(i)
        there = pz * heads + py
        return pltpu.make_async_remote_copy(
            src_ref=out_ret.at[pl.ds(pl.multiple_of(there * unit, unit), unit)],
            dst_ref=in_ret.at[pl.ds(own_src, unit)],
            send_sem=ret_send,
            recv_sem=ret_recv.at[y],
            device_id=(there, mp),
            device_id_type=MESH,
        )

    def send_ret(i, carry):
        ret_copy(i).start()
        return carry

    lax.fori_loop(0, devices - 1, send_ret, 0)
    pltpu.make_async_copy(
        out_ret.at[pl.ds(own_dst, unit)], in_ret.at[pl.ds(own_src, unit)], ret_recv.at[y]
    ).start()

    load_w.wait()
    for h in range(heads):
        here = in_ret.at[h * slots : (h + 1) * slots]
        pltpu.make_async_copy(here, here, ret_recv.at[h]).wait()
        tok_buf[:, h * dim : (h + 1) * dim] = dot(pick_buf[h], here[...]).astype(BF16)

    def share_of(m):
        return dot(tok_buf[...], w_buf[:, pl.ds(pl.multiple_of(m * block, block), block)])

    offsets = sorted(range(chips), key=lambda off: -min(off, chips - off))
    for k, off in enumerate(offsets):
        cx = lax.rem(x + off, chips)
        pair_out[k] = share_of(cx * 2 + 1 - core).astype(BF16)
        pltpu.make_async_remote_copy(
            src_ref=pair_out.at[k],
            dst_ref=pair_in.at[k],
            send_sem=pair_send,
            recv_sem=pair_recv.at[k],
            device_id=(me, x * 2 + 1 - core),
            device_id_type=MESH,
        ).start()
    total = None
    for k, off in enumerate(offsets):
        cx = lax.rem(x + off, chips)
        total = share_of(cx * 2 + core)
        pltpu.make_async_copy(pair_in.at[k], pair_in.at[k], pair_recv.at[k]).wait()
        total = total + pair_in[k].astype(F32)
        if off:
            chip_out[k] = total.astype(BF16)
            pltpu.make_async_remote_copy(
                src_ref=chip_out.at[k],
                dst_ref=chip_in.at[k],
                send_sem=chip_send,
                recv_sem=chip_recv.at[k],
                device_id=(me, cx * 2 + core),
                device_id_type=MESH,
            ).start()
    for k in range(chips - 1):
        pltpu.make_async_copy(chip_in.at[k], chip_in.at[k], chip_recv.at[k]).wait()
        total = total + chip_in[k].astype(F32)
    out_ref[...] = total.astype(BF16)

    most = (devices - 1) * unit
    pltpu.make_async_copy(out_pack.at[:most], out_pack.at[:most], pack_send).wait()
    pltpu.make_async_copy(prev_buf, prev_buf, next_send).wait()
    pltpu.make_async_copy(out_ret.at[:most], out_ret.at[:most], ret_send).wait()
    pltpu.make_async_copy(pair_out, pair_out, pair_send).wait()
    pltpu.make_async_copy(chip_out, chip_out, chip_send).wait()


def local(planes, chips, shared_qk, values, buckets, counts, w_out):
    tok, width = shared_qk.shape
    heads = buckets.shape[1]
    dim = width // heads
    devices = planes * heads
    slots = devices * CAP
    groups = devices // 16
    block = w_out.shape[1] // (2 * chips)
    vmem = pl.BlockSpec(memory_space=pltpu.VMEM)
    dma = pltpu.SemaphoreType.DMA
    return pl.pallas_call(
        functools.partial(layer_kernel, planes, heads, chips, tok, dim),
        out_shape=jax.ShapeDtypeStruct((tok, block), BF16),
        in_specs=[vmem, vmem, vmem, vmem, pl.BlockSpec(memory_space=pl.ANY)],
        out_specs=vmem,
        scratch_shapes=[
            pltpu.VMEM(w_out.shape, BF16),
            pltpu.VMEM((heads * slots, 2 * dim), BF16),
            pltpu.VMEM((heads * slots, 2 * dim), BF16),
            pltpu.VMEM((heads, slots, 2 * dim), BF16),
            pltpu.VMEM((slots, 2 * dim), BF16),
            pltpu.VMEM((heads, slots, dim), BF16),
            pltpu.VMEM((heads * slots, dim), BF16),
            pltpu.VMEM((heads * slots, dim), BF16),
            pltpu.VMEM((tok, heads * dim), BF16),
            pltpu.VMEM((heads, tok, slots), BF16),
            pltpu.VMEM((chips, tok, block), BF16),
            pltpu.VMEM((chips, tok, block), BF16),
            pltpu.VMEM((chips - 1, tok, block), BF16),
            pltpu.VMEM((chips - 1, tok, block), BF16),
            dma,
            dma,
            dma((groups,)),
            dma,
            dma,
            dma,
            dma((heads,)),
            dma,
            dma((chips,)),
            dma,
            dma((chips - 1,)),
        ],
        compiler_params=pltpu.CompilerParams(
            collective_id=0, has_side_effects=True, vmem_limit_bytes=32 * 1024 * 1024
        ),
    )(shared_qk, values, buckets, counts, w_out)


def solution(mesh):
    placed = (P("seq", "mp"), P("seq", "mp"), P("seq", "mp"), P(None, "mp", None), P("mp", None))
    heads = 4
    planes = mesh.shape["seq"] // heads
    chips = mesh.shape["mp"] // 2
    return jax.shard_map(
        functools.partial(local, planes, chips),
        mesh=mesh, in_specs=placed, out_specs=P("seq", "mp"), check_vma=False,
    )
```

time: 194 us -> 80.7 us (0.42)
  waiting for transfers between devices: 91.7 us -> 0 us
  Pallas kernels: 0 us -> 74.1 us
  local copies, waits for them, and re-layouts: 39.8 us -> 6.34 us
  starting transfers between devices: 30.6 us -> 0 us
  between operations: 13.7 us -> 0.02 us
  other arithmetic: 9.82 us -> 0 us
  matrix products: 7.33 us -> 0 us
    pallas_call x0 -> x1, Pallas kernels: none -> 74.1 us  [local(): pl.pallas_call(functools.partial(layer_kernel, planes, heads, chips, tok,...]
    all_to_all x2 -> x0, waiting for transfers between devices: 45.2 us -> none  [the longest x1 28 us: local(): lax.all_to_all(outgoing, 'seq', split_axis=0, concat_axis=0, tiled=True)]
    gather x8 -> x0, local copies, waits for them, and re-layouts: 37.1 us -> none  [the longest x2 8.96 us: local(): token_order[head_range[None, :, None], jnp.minimum(send_index, tok_rows -...]
    reduce_scatter x1 -> x0, waiting for transfers between devices: 35.4 us -> none  [local(): lax.psum_scatter(partial_sum, 'mp', scatter_dimension=1, tiled=True)]
    all_to_all x2 -> x0, starting transfers between devices: 27 us -> none  [the longest x1 19.3 us: local(): lax.all_to_all(outgoing, 'seq', split_axis=0, concat_axis=0, tiled=True)]
    ppermute x1 -> x0, waiting for transfers between devices: 11.1 us -> none  [passed_along(): lax.ppermute(shard, axis, [(i, (i + by) % devices) for i in range(devices)])]
    dot_general x9 -> x0, matrix products: 7.33 us -> none  [the longest x1 4.26 us: local(): partial_sum = jnp.dot(token_out, w_out, preferred_element_type=jnp.float32)]
    unnamed x11 -> x10, local copies, waits for them, and re-layouts: 0.52 us -> 6.34 us
  transfers between devices with their start and end apart: 4 -> 0, of which waited for: 4 -> 0; matrix products, arithmetic and copies ran while one was open for 1% -> 0% of each run, Pallas kernels for 0% -> 0%
where the time goes in v1:
time: 80.7 us; the launch traced here: 80.5 us
  Pallas kernels  74.1 us (92%)
  local copies, waits for them, and re-layouts  6.34 us (8%)
    pallas_call x1, Pallas kernels, local(): pl.pallas_call(functools.partial(layer_kernel, planes, heads, chips, tok,...  74.1 us
    unnamed x10, local copies, waits for them, and re-layouts  6.34 us

profile of v1, /device:TPU:1, one launch (start us, length us, event | category | flops | bytes accessed | tf_op | source)
XLA Modules:
  0.0 80.5 jit_solution(17411395856656235793)
XLA Ops:
  0.0 0.8 copy.6.buckets_ref
  0.8 0.0 copy-start
  0.8 2.2 %copy-done = bf16[512,4096]{1,0:T(8,128)(2,1)S(1)} copy-done((bf16[512,4096]{1,0:T(8,128)(2,1)S(1)}, bf16[512,4096]{1,0:T(8,128)(2,1)}, u32[]{:S(2)}) %copy-start) | copy-done | bytes 4194328
  3.0 0.0 copy-start.1
  3.0 0.9 %copy-done.1 = bf16[128,512]{1,0:T(8,128)(2,1)S(1)} copy-done((bf16[128,512]{1,0:T(8,128)(2,1)S(1)}, bf16[128,512]{1,0:T(8,128)(2,1)}, u32[]{:S(2)}) %copy-start.1) | copy-done | bytes 131096
  3.9 0.0 copy-start.2
  3.9 0.9 %copy-done.2 = bf16[128,512]{1,0:T(8,128)(2,1)S(1)} copy-done((bf16[128,512]{1,0:T(8,128)(2,1)S(1)}, bf16[128,512]{1,0:T(8,128)(2,1)}, u32[]{:S(2)}) %copy-start.2) | copy-done | bytes 131096
  4.8 0.0 copy-start.3
  4.8 0.9 %copy-done.3 = s32[64,4,64]{2,1,0:T(4,128)S(1)} copy-done((s32[64,4,64]{2,1,0:T(4,128)S(1)}, s32[64,4,64]{2,1,0:T(4,128)}, u32[]{:S(2)}) %copy-start.3) | copy-done | bytes 65560
  5.7 74.1 %shard_map.55 = bf16[128,512]{1,0:T(8,128)(2,1)S(1)} custom-call(bf16[128,512]{1,0:T(8,128)(2,1)S(1)} %copy-done.1, bf16[128,512]{1,0:T(8,128)(2,1)S(1)} %copy-done.2, s32[128,4]{1,0:T(8,128)S(1)} %copy.6.buckets_ref, s32[64,4,64]{2,1,0:T(4,128)S(1)} %copy-done.3, bf16[512,4096]{1,0:T(8,128)(2,1)S(1)} %copy-done), custom_call_target="tpu_custom_call" | custom-call | tf_op jit(solution)/shard_map/pallas_call | solution.py:259
  79.8 0.7 copy.8
Async XLA Ops:
  0.8 2.2 %copy-start = (bf16[512,4096]{1,0:T(8,128)(2,1)S(1)}, bf16[512,4096]{1,0:T(8,128)(2,1)}, u32[]{:S(2)}) copy-start(bf16[512,4096]{1,0:T(8,128)(2,1)} %w_ref.1) | copy-start | bytes 12582916
  3.0 0.9 %copy-start.1 = (bf16[128,512]{1,0:T(8,128)(2,1)S(1)}, bf16[128,512]{1,0:T(8,128)(2,1)}, u32[]{:S(2)}) copy-start(bf16[128,512]{1,0:T(8,128)(2,1)} %qk_ref.1) | copy-start | bytes 393220
  3.9 0.9 %copy-start.2 = (bf16[128,512]{1,0:T(8,128)(2,1)S(1)}, bf16[128,512]{1,0:T(8,128)(2,1)}, u32[]{:S(2)}) copy-start(bf16[128,512]{1,0:T(8,128)(2,1)} %val_ref.1) | copy-start | bytes 393220
  4.8 0.9 %copy-start.3 = (s32[64,4,64]{2,1,0:T(4,128)S(1)}, s32[64,4,64]{2,1,0:T(4,128)}, u32[]{:S(2)}) copy-start(s32[64,4,64]{2,1,0:T(4,128)} %counts_ref.1) | copy-start | bytes 196612

commit v2 on v1

--- a/solution.py
+++ b/solution.py
@@ -30,10 +30,10 @@
 
 def layer_kernel(
     planes, heads, chips, tok, dim,
-    qk_ref, val_ref, buckets_ref, counts_ref, w_ref, out_ref,
-    w_buf, out_pack, in_pack, rows_buf, prev_buf, att_buf, out_ret, in_ret, tok_buf, pick_buf,
+    qk_hbm, val_hbm, buckets_hbm, counts_hbm, w_hbm, out_ref,
+    qk_ref, val_ref, buckets_ref, counts_ref, w_buf, out_pack, in_pack, rows_buf, prev_buf, att_buf, out_ret, in_ret, tok_buf, pick_buf,
     pair_out, pair_in, chip_out, chip_in,
-    w_sem, pack_send, pack_recv, next_send, next_recv, ret_send, ret_recv,
+    load_sem, w_sem, pack_send, pack_recv, next_send, next_recv, ret_send, ret_recv,
     pair_send, pair_recv, chip_send, chip_recv,
 ):
     devices = planes * heads
@@ -42,14 +42,21 @@
     groups = devices // 16
     span = 16 * unit
     part = 16 * CAP
-    block = w_ref.shape[1] // (2 * chips)
+    block = w_hbm.shape[1] // (2 * chips)
     me = lax.axis_index("seq")
     mp = lax.axis_index("mp")
     z, y = me // heads, lax.rem(me, heads)
     x, core = mp // 2, lax.rem(mp, 2)
 
-    load_w = pltpu.make_async_copy(w_ref, w_buf, w_sem)
-    load_w.start()
+    loads = [
+        pltpu.make_async_copy(buckets_hbm, buckets_ref, load_sem.at[0]),
+        pltpu.make_async_copy(qk_hbm, qk_ref, load_sem.at[1]),
+        pltpu.make_async_copy(val_hbm, val_ref, load_sem.at[2]),
+        pltpu.make_async_copy(counts_hbm, counts_ref, load_sem.at[3]),
+        pltpu.make_async_copy(w_hbm, w_buf, w_sem),
+    ]
+    for load in loads:
+        load.start()
 
     barrier = pltpu.get_barrier_semaphore()
 
@@ -66,15 +73,14 @@
 
     eye = iota((tok, tok), 0) == iota((tok, tok), 1)
     before = iota((tok, tok), 0) < iota((tok, tok), 1)
-    after = iota((tok, tok), 0) > iota((tok, tok), 1)
+    for load in loads[:3]:
+        load.wait()
     for h in range(heads):
-        b_col = buckets_ref[:, h : h + 1]
-        b_row = jnp.sum(jnp.where(eye, b_col, 0), axis=0, keepdims=True)
+        b_row = buckets_ref[h : h + 1, :]
+        b_col = jnp.sum(jnp.where(eye, b_row, 0), axis=1, keepdims=True)
         same = b_col == b_row
         rank_row = jnp.sum(jnp.where(same & before, 1, 0), axis=0, keepdims=True)
-        rank_col = jnp.sum(jnp.where(same & after, 1, 0), axis=1, keepdims=True)
         place = one_hot(iota((slots, tok), 0) == b_row * CAP + rank_row)
-        pick_buf[h] = one_hot(iota((tok, slots), 1) == b_col * CAP + rank_col)
         cols = slice(h * dim, (h + 1) * dim)
         rows = slice(h * slots, (h + 1) * slots)
         out_pack[rows, :dim] = dot(place, qk_ref[:, cols]).astype(BF16)
@@ -114,6 +120,13 @@
         out_pack.at[pl.ds(own_src, unit)], in_pack.at[pl.ds(own_dst, unit)], pack_recv.at[me // 16]
     ).start()
 
+    after = iota((tok, tok), 0) > iota((tok, tok), 1)
+    for h in range(heads):
+        b_row = buckets_ref[h : h + 1, :]
+        b_col = jnp.sum(jnp.where(eye, b_row, 0), axis=1, keepdims=True)
+        rank_col = jnp.sum(jnp.where((b_col == b_row) & after, 1, 0), axis=1, keepdims=True)
+        pick_buf[h] = one_hot(iota((tok, slots), 1) == b_col * CAP + rank_col)
+    loads[3].wait()
     counts = counts_ref[:, y, :]
     spread = (iota((devices, slots), 1) // CAP) == iota((devices, slots), 0)
     rank = lax.rem(iota((1, slots), 1), CAP)
@@ -150,12 +163,16 @@
     itself = iota((slots, slots), 0) == iota((slots, slots), 1)
     scale = 1.0 / math.sqrt(dim)
 
-    def attend(j, prev):
+    trans = (((1,), (1,)), ((), ()))
+
+    def own_scores(j):
+        q = rows_buf[j, :, :dim]
+        own = lax.dot_general(q, q, trans, preferred_element_type=F32)
+        return jnp.where(itself, SELF_SCORE, own * scale + dead[j + 1])
+
+    def attend(j, own, prev):
         q = rows_buf[j, :, :dim]
         v = rows_buf[j, :, dim:]
-        trans = (((1,), (1,)), ((), ()))
-        own = lax.dot_general(q, q, trans, preferred_element_type=F32)
-        own = jnp.where(itself, SELF_SCORE, own * scale + dead[j + 1])
         far = lax.dot_general(q, prev[:, :dim], trans, preferred_element_type=F32) * scale + dead[j]
         top = jnp.maximum(jnp.max(own, axis=1, keepdims=True), jnp.max(far, axis=1, keepdims=True))
         own = jnp.exp(own - top)
@@ -166,9 +183,10 @@
         att_buf[j] = att.astype(BF16)
 
     for j in range(1, heads):
-        attend(j, rows_buf[j - 1])
+        attend(j, own_scores(j), rows_buf[j - 1])
+    own = own_scores(0)
     pltpu.make_async_copy(prev_buf, prev_buf, next_recv).wait()
-    attend(0, prev_buf[...])
+    attend(0, own, prev_buf[...])
 
     for g in range(groups):
         rows = slice(g * part, (g + 1) * part)
@@ -196,7 +214,7 @@
         out_ret.at[pl.ds(own_dst, unit)], in_ret.at[pl.ds(own_src, unit)], ret_recv.at[y]
     ).start()
 
-    load_w.wait()
+    loads[4].wait()
     for h in range(heads):
         here = in_ret.at[h * slots : (h + 1) * slots]
         pltpu.make_async_copy(here, here, ret_recv.at[h]).wait()
@@ -205,9 +223,23 @@
     def share_of(m):
         return dot(tok_buf[...], w_buf[:, pl.ds(pl.multiple_of(m * block, block), block)])
 
-    offsets = sorted(range(chips), key=lambda off: -min(off, chips - off))
-    for k, off in enumerate(offsets):
-        cx = lax.rem(x + off, chips)
+    ways = (2, 1, 3, 0)
+    half = tok // 2
+
+    def to_chip(k, src, way):
+        cx = lax.rem(x + way, chips)
+        copy = pltpu.make_async_remote_copy(
+            src_ref=src,
+            dst_ref=chip_in.at[k],
+            send_sem=chip_send,
+            recv_sem=chip_recv.at[k],
+            device_id=(me, cx * 2 + core),
+            device_id_type=MESH,
+        )
+        copy.start()
+
+    def give(k):
+        cx = lax.rem(x + ways[k], chips)
         pair_out[k] = share_of(cx * 2 + 1 - core).astype(BF16)
         pltpu.make_async_remote_copy(
             src_ref=pair_out.at[k],
@@ -217,26 +249,39 @@
             device_id=(me, x * 2 + 1 - core),
             device_id_type=MESH,
         ).start()
-    total = None
-    for k, off in enumerate(offsets):
-        cx = lax.rem(x + off, chips)
-        total = share_of(cx * 2 + core)
+
+    def pair_sum(k):
+        cx = lax.rem(x + ways[k], chips)
+        mine = share_of(cx * 2 + core)
         pltpu.make_async_copy(pair_in.at[k], pair_in.at[k], pair_recv.at[k]).wait()
-        total = total + pair_in[k].astype(F32)
-        if off:
-            chip_out[k] = total.astype(BF16)
-            pltpu.make_async_remote_copy(
-                src_ref=chip_out.at[k],
-                dst_ref=chip_in.at[k],
-                send_sem=chip_send,
-                recv_sem=chip_recv.at[k],
-                device_id=(me, cx * 2 + core),
-                device_id_type=MESH,
-            ).start()
-    for k in range(chips - 1):
+        return mine + pair_in[k].astype(F32)
+
+    def arrived(k):
         pltpu.make_async_copy(chip_in.at[k], chip_in.at[k], chip_recv.at[k]).wait()
-        total = total + chip_in[k].astype(F32)
-    out_ref[...] = total.astype(BF16)
+        return chip_in[k].astype(F32)
+
+    def put(k, rows, way):
+        chip_out[k] = rows.astype(BF16)
+        to_chip(k, chip_out.at[k], way)
+
+    give(0)
+    give(1)
+    opposite = pair_sum(0)
+    put(0, opposite[:half], 1)
+    put(1, opposite[half:], 3)
+    give(2)
+    right = pair_sum(1)
+    put(2, right[half:], 1)
+    give(3)
+    left = pair_sum(2)
+    put(3, left[:half], 3)
+    put(4, right[:half] + arrived(0), 1)
+    put(5, left[half:] + arrived(1), 3)
+    total = pair_sum(3)
+    upper = total[:half] + arrived(3)
+    lower = total[half:] + arrived(2)
+    out_ref[:half, :] = (upper + arrived(4)).astype(BF16)
+    out_ref[half:, :] = (lower + arrived(5)).astype(BF16)
 
     most = (devices - 1) * unit
     pltpu.make_async_copy(out_pack.at[:most], out_pack.at[:most], pack_send).wait()
@@ -247,8 +292,9 @@
 
 
 def local(planes, chips, shared_qk, values, buckets, counts, w_out):
+    buckets = buckets.T
     tok, width = shared_qk.shape
-    heads = buckets.shape[1]
+    heads = buckets.shape[0]
     dim = width // heads
     devices = planes * heads
     slots = devices * CAP
@@ -259,9 +305,13 @@
     return pl.pallas_call(
         functools.partial(layer_kernel, planes, heads, chips, tok, dim),
         out_shape=jax.ShapeDtypeStruct((tok, block), BF16),
-        in_specs=[vmem, vmem, vmem, vmem, pl.BlockSpec(memory_space=pl.ANY)],
+        in_specs=[pl.BlockSpec(memory_space=pl.ANY)] * 5,
         out_specs=vmem,
         scratch_shapes=[
+            pltpu.VMEM(shared_qk.shape, BF16),
+            pltpu.VMEM(values.shape, BF16),
+            pltpu.VMEM(buckets.shape, jnp.int32),
+            pltpu.VMEM(counts.shape, jnp.int32),
             pltpu.VMEM(w_out.shape, BF16),
             pltpu.VMEM((heads * slots, 2 * dim), BF16),
             pltpu.VMEM((heads * slots, 2 * dim), BF16),
@@ -274,8 +324,9 @@
             pltpu.VMEM((heads, tok, slots), BF16),
             pltpu.VMEM((chips, tok, block), BF16),
             pltpu.VMEM((chips, tok, block), BF16),
-            pltpu.VMEM((chips - 1, tok, block), BF16),
-            pltpu.VMEM((chips - 1, tok, block), BF16),
+            pltpu.VMEM((6, tok // 2, block), BF16),
+            pltpu.VMEM((6, tok // 2, block), BF16),
+            dma((4,)),
             dma,
             dma,
             dma((groups,)),
@@ -286,10 +337,10 @@
             dma,
             dma((chips,)),
             dma,
-            dma((chips - 1,)),
+            dma((6,)),
         ],
         compiler_params=pltpu.CompilerParams(
-            collective_id=0, has_side_effects=True, vmem_limit_bytes=32 * 1024 * 1024
+            collective_id=0, has_side_effects=True, vmem_limit_bytes=60 * 1024 * 1024
         ),
     )(shared_qk, values, buckets, counts, w_out)
 

time: 80.7 us -> 75 us (0.929)
  local copies, waits for them, and re-layouts: 6.34 us -> 1.57 us
    unnamed x10 -> x1, local copies, waits for them, and re-layouts: 6.34 us -> 1.57 us
    pallas_call x1, Pallas kernels: 74.1 us -> 73.3 us  [local(): pl.pallas_call(functools.partial(layer_kernel, planes, heads, chips, tok,...]
where the time goes in v2:
time: 75 us; the launch traced here: 74.9 us
  Pallas kernels  73.3 us (98%)
  local copies, waits for them, and re-layouts  1.57 us (2%)
    pallas_call x1, Pallas kernels, local(): pl.pallas_call(functools.partial(layer_kernel, planes, heads, chips, tok,...  73.3 us
    unnamed x1, local copies, waits for them, and re-layouts  1.57 us

profile of v2, /device:TPU:1, one launch (start us, length us, event | category | flops | bytes accessed | tf_op | source)
XLA Modules:
  0.0 74.9 jit_solution(12367048993552362317)
XLA Ops:
  0.0 73.3 %shard_map.55 = bf16[128,512]{1,0:T(8,128)(2,1)} custom-call(bf16[128,512]{1,0:T(8,128)(2,1)} %qk_hbm.1, bf16[128,512]{1,0:T(8,128)(2,1)} %val_hbm.1, s32[4,128]{1,0:T(4,128)} %bitcast.1, s32[64,4,64]{2,1,0:T(4,128)} %counts_hbm.1, bf16[512,4096]{1,0:T(8,128)(2,1)} %w_hbm.1), custom_call_target="tpu_custom_call" | custom-call | tf_op jit(solution)/shard_map/pallas_call | solution.py:305
  73.3 1.6 %copy.7 = bf16[128,512]{1,0:T(8,128)(2,1)} copy(bf16[128,512]{1,0:T(8,128)(2,1)} %shard_map.55) | data formatting | bytes 262144

commit v3 on v2

--- a/solution.py
+++ b/solution.py
@@ -73,18 +73,21 @@
 
     eye = iota((tok, tok), 0) == iota((tok, tok), 1)
     before = iota((tok, tok), 0) < iota((tok, tok), 1)
+    out_row = iota((slots, 2 * tok), 0)
+    wanted = out_row // unit * unit + out_row % (unit // 2) + out_row // (unit // 2) % 2 * slots
     for load in loads[:3]:
         load.wait()
     for h in range(heads):
         b_row = buckets_ref[h : h + 1, :]
         b_col = jnp.sum(jnp.where(eye, b_row, 0), axis=1, keepdims=True)
-        same = b_col == b_row
-        rank_row = jnp.sum(jnp.where(same & before, 1, 0), axis=0, keepdims=True)
-        place = one_hot(iota((slots, tok), 0) == b_row * CAP + rank_row)
+        rank_row = jnp.sum(jnp.where((b_col == b_row) & before, 1, 0), axis=0, keepdims=True)
+        slot_row = b_row * CAP + rank_row
+        slot_row = jnp.concatenate([slot_row, slot_row + slots], axis=1)
         cols = slice(h * dim, (h + 1) * dim)
-        rows = slice(h * slots, (h + 1) * slots)
-        out_pack[rows, :dim] = dot(place, qk_ref[:, cols]).astype(BF16)
-        out_pack[rows, dim:] = dot(place, val_ref[:, cols]).astype(BF16)
+        tokens = jnp.concatenate([qk_ref[:, cols], val_ref[:, cols]], axis=0)
+        for p in range(2):
+            place = one_hot(wanted + (unit // 2 if p == 0 else 0) == slot_row)
+            out_pack[p, h * slots : (h + 1) * slots, :] = dot(place, tokens).astype(BF16)
 
     pl.semaphore_wait(barrier, devices - 1 + chips)
 
@@ -96,29 +99,32 @@
         py = lax.rem(y + heads - 1 - lax.rem(i, heads), heads)
         return pz, py
 
-    def pack_copy(i):
+    def pack_copy(p, i):
         pz, py = peer(i)
         src = pl.multiple_of(py * slots + pz * unit, unit)
         dst = pl.multiple_of(me * unit, unit)
         return pltpu.make_async_remote_copy(
-            src_ref=out_pack.at[pl.ds(src, unit)],
-            dst_ref=in_pack.at[pl.ds(dst, unit)],
-            send_sem=pack_send,
-            recv_sem=pack_recv.at[me // 16],
+            src_ref=out_pack.at[p, pl.ds(src, unit)],
+            dst_ref=in_pack.at[p, pl.ds(dst, unit)],
+            send_sem=pack_send.at[p],
+            recv_sem=pack_recv.at[p, me // 16],
             device_id=(pz * heads + py, mp),
             device_id_type=MESH,
         )
 
-    def send_pack(i, carry):
-        pack_copy(i).start()
-        return carry
-
-    lax.fori_loop(0, devices - 1, send_pack, 0)
     own_src = pl.multiple_of(y * slots + z * unit, unit)
     own_dst = pl.multiple_of(me * unit, unit)
-    pltpu.make_async_copy(
-        out_pack.at[pl.ds(own_src, unit)], in_pack.at[pl.ds(own_dst, unit)], pack_recv.at[me // 16]
-    ).start()
+    for p in range(2):
+        def send_pack(i, carry, p=p):
+            pack_copy(p, i).start()
+            return carry
+
+        lax.fori_loop(0, devices - 1, send_pack, 0)
+        pltpu.make_async_copy(
+            out_pack.at[p, pl.ds(own_src, unit)],
+            in_pack.at[p, pl.ds(own_dst, unit)],
+            pack_recv.at[p, me // 16],
+        ).start()
 
     after = iota((tok, tok), 0) > iota((tok, tok), 1)
     for h in range(heads):
@@ -138,78 +144,86 @@
         dead.append(jnp.where(rank < row, 0.0, DEAD))
 
     def by_bucket(i):
-        return (i // CAP) % 16 * unit + i // part * CAP + i % CAP
+        return i // CAP % 16 * unit + i // part // 2 * (unit // 2) + i // part % 2 * CAP + i % CAP
 
     order = one_hot(by_bucket(iota((span, span), 0)) == iota((span, span), 1))
-    order_back = one_hot(by_bucket(iota((span, span), 1)) == iota((span, span), 0))
-
+
+    def by_source(i):
+        return i // CAP % 16 * unit + i // part * CAP + i % CAP
+
+    order_back = one_hot(by_source(iota((span, span), 1)) == iota((span, span), 0))
+
+    def receive(p):
+        for g in range(groups):
+            here = in_pack.at[p, g * span : (g + 1) * span]
+            pltpu.make_async_copy(here, here, pack_recv.at[p, g]).wait()
+            arranged = dot(order, here[...]).astype(BF16)
+            for n in range(4):
+                j = n % 2 + (heads // 2 if p == 0 else 0)
+                rows_buf[j, n // 2, g * part : (g + 1) * part, :] = arranged[n * part : (n + 1) * part]
+
+    receive(0)
     next_z = lax.rem(z + 1, planes)
-    for g in range(groups):
-        here = in_pack.at[g * span : (g + 1) * span]
-        pltpu.make_async_copy(here, here, pack_recv.at[g]).wait()
-        arranged = dot(order, here[...]).astype(BF16)
-        rows = slice(g * part, (g + 1) * part)
-        for j in range(heads):
-            rows_buf[j, rows, :] = arranged[j * part : (j + 1) * part]
-        pltpu.make_async_remote_copy(
-            src_ref=rows_buf.at[heads - 1, rows],
-            dst_ref=prev_buf.at[rows],
-            send_sem=next_send,
-            recv_sem=next_recv,
-            device_id=(next_z * heads + y, mp),
-            device_id_type=MESH,
-        ).start()
-
-    itself = iota((slots, slots), 0) == iota((slots, slots), 1)
+    to_next = pltpu.make_async_remote_copy(
+        src_ref=rows_buf.at[heads - 1],
+        dst_ref=prev_buf,
+        send_sem=next_send,
+        recv_sem=next_recv,
+        device_id=(next_z * heads + y, mp),
+        device_id_type=MESH,
+    )
+    to_next.start()
+
     scale = 1.0 / math.sqrt(dim)
-
     trans = (((1,), (1,)), ((), ()))
 
-    def own_scores(j):
-        q = rows_buf[j, :, :dim]
-        own = lax.dot_general(q, q, trans, preferred_element_type=F32)
-        return jnp.where(itself, SELF_SCORE, own * scale + dead[j + 1])
-
-    def attend(j, own, prev):
-        q = rows_buf[j, :, :dim]
-        v = rows_buf[j, :, dim:]
-        far = lax.dot_general(q, prev[:, :dim], trans, preferred_element_type=F32) * scale + dead[j]
+    def attend(j, prev, first, count):
+        rows = slice(first, first + count)
+        itself = iota((count, slots), 0) + first == iota((count, slots), 1)
+        q = rows_buf[j, 0, rows, :]
+        own = lax.dot_general(q, rows_buf[j, 0], trans, preferred_element_type=F32)
+        own = jnp.where(itself, SELF_SCORE, own * scale + dead[j + 1])
+        far = lax.dot_general(q, prev[0], trans, preferred_element_type=F32) * scale + dead[j]
         top = jnp.maximum(jnp.max(own, axis=1, keepdims=True), jnp.max(far, axis=1, keepdims=True))
         own = jnp.exp(own - top)
         far = jnp.exp(far - top)
         total = jnp.sum(own, axis=1, keepdims=True) + jnp.sum(far, axis=1, keepdims=True)
         share = 1.0 / total
-        att = dot((own * share).astype(BF16), v) + dot((far * share).astype(BF16), prev[:, dim:])
-        att_buf[j] = att.astype(BF16)
-
-    for j in range(1, heads):
-        attend(j, own_scores(j), rows_buf[j - 1])
-    own = own_scores(0)
-    pltpu.make_async_copy(prev_buf, prev_buf, next_recv).wait()
-    attend(0, own, prev_buf[...])
-
-    for g in range(groups):
-        rows = slice(g * part, (g + 1) * part)
-        mine = jnp.concatenate([att_buf[j, rows, :] for j in range(heads)], axis=0)
-        out_ret[g * span : (g + 1) * span, :] = dot(order_back, mine).astype(BF16)
-
-    def ret_copy(i):
-        pz, py = peer(i)
-        there = pz * heads + py
-        return pltpu.make_async_remote_copy(
-            src_ref=out_ret.at[pl.ds(pl.multiple_of(there * unit, unit), unit)],
-            dst_ref=in_ret.at[pl.ds(own_src, unit)],
-            send_sem=ret_send,
-            recv_sem=ret_recv.at[y],
-            device_id=(there, mp),
-            device_id_type=MESH,
-        )
-
-    def send_ret(i, carry):
-        ret_copy(i).start()
-        return carry
-
-    lax.fori_loop(0, devices - 1, send_ret, 0)
+        att = dot((own * share).astype(BF16), rows_buf[j, 1]) + dot((far * share).astype(BF16), prev[1])
+        att_buf[j, rows, :] = att.astype(BF16)
+
+    attend(heads - 1, rows_buf.at[heads - 2], 0, slots)
+    receive(1)
+    to_next.wait_recv()
+
+    def send_ret(c):
+        def body(i, carry):
+            pz, py = peer(i)
+            there = pz * heads + py
+
+            @pl.when(pz // (planes // 2) == c)
+            def _():
+                pltpu.make_async_remote_copy(
+                    src_ref=out_ret.at[pl.ds(pl.multiple_of(there * unit, unit), unit)],
+                    dst_ref=in_ret.at[pl.ds(own_src, unit)],
+                    send_sem=ret_send,
+                    recv_sem=ret_recv.at[y],
+                    device_id=(there, mp),
+                    device_id_type=MESH,
+                ).start()
+
+            return carry
+
+        lax.fori_loop(0, devices - 1, body, 0)
+
+    for c in range(2):
+        for j in range(heads - 1):
+            attend(j, rows_buf.at[j - 1] if j else prev_buf, c * slots // 2, slots // 2)
+        for g in range(c * groups // 2, (c + 1) * groups // 2):
+            rows = slice(g * part, (g + 1) * part)
+            mine = jnp.concatenate([att_buf[j, rows, :] for j in range(heads)], axis=0)
+            out_ret[g * span : (g + 1) * span, :] = dot(order_back, mine).astype(BF16)
+        send_ret(c)
     pltpu.make_async_copy(
         out_ret.at[pl.ds(own_dst, unit)], in_ret.at[pl.ds(own_src, unit)], ret_recv.at[y]
     ).start()
@@ -284,8 +298,9 @@
     out_ref[half:, :] = (lower + arrived(5)).astype(BF16)
 
     most = (devices - 1) * unit
-    pltpu.make_async_copy(out_pack.at[:most], out_pack.at[:most], pack_send).wait()
-    pltpu.make_async_copy(prev_buf, prev_buf, next_send).wait()
+    for p in range(2):
+        pltpu.make_async_copy(out_pack.at[p, :most], out_pack.at[p, :most], pack_send.at[p]).wait()
+    to_next.wait_send()
     pltpu.make_async_copy(out_ret.at[:most], out_ret.at[:most], ret_send).wait()
     pltpu.make_async_copy(pair_out, pair_out, pair_send).wait()
     pltpu.make_async_copy(chip_out, chip_out, chip_send).wait()
@@ -313,10 +328,10 @@
             pltpu.VMEM(buckets.shape, jnp.int32),
             pltpu.VMEM(counts.shape, jnp.int32),
             pltpu.VMEM(w_out.shape, BF16),
-            pltpu.VMEM((heads * slots, 2 * dim), BF16),
-            pltpu.VMEM((heads * slots, 2 * dim), BF16),
-            pltpu.VMEM((heads, slots, 2 * dim), BF16),
-            pltpu.VMEM((slots, 2 * dim), BF16),
+            pltpu.VMEM((2, heads * slots, dim), BF16),
+            pltpu.VMEM((2, heads * slots, dim), BF16),
+            pltpu.VMEM((heads, 2, slots, dim), BF16),
+            pltpu.VMEM((2, slots, dim), BF16),
             pltpu.VMEM((heads, slots, dim), BF16),
             pltpu.VMEM((heads * slots, dim), BF16),
             pltpu.VMEM((heads * slots, dim), BF16),
@@ -328,8 +343,8 @@
             pltpu.VMEM((6, tok // 2, block), BF16),
             dma((4,)),
             dma,
-            dma,
-            dma((groups,)),
+            dma((2,)),
+            dma((2, groups)),
             dma,
             dma,
             dma,

time: 75 us -> 71.6 us (0.955)
  Pallas kernels: 73.3 us -> 69.9 us
    pallas_call x1, Pallas kernels: 73.3 us -> 69.9 us  [local(): pl.pallas_call(functools.partial(layer_kernel, planes, heads, chips, tok,...]
where the time goes in v3:
time: 71.6 us; the launch traced here: 71.4 us
  Pallas kernels  69.9 us (98%)
  local copies, waits for them, and re-layouts  1.57 us (2%)
    pallas_call x1, Pallas kernels, local(): pl.pallas_call(functools.partial(layer_kernel, planes, heads, chips, tok,...  69.9 us
    unnamed x1, local copies, waits for them, and re-layouts  1.57 us

profile of v3, /device:TPU:1, one launch (start us, length us, event | category | flops | bytes accessed | tf_op | source)
XLA Modules:
  0.0 71.4 jit_solution(61080437170368792)
XLA Ops:
  0.0 69.9 %shard_map.55 = bf16[128,512]{1,0:T(8,128)(2,1)} custom-call(bf16[128,512]{1,0:T(8,128)(2,1)} %qk_hbm.1, bf16[128,512]{1,0:T(8,128)(2,1)} %val_hbm.1, s32[4,128]{1,0:T(4,128)} %bitcast.1, s32[64,4,64]{2,1,0:T(4,128)} %counts_hbm.1, bf16[512,4096]{1,0:T(8,128)(2,1)} %w_hbm.1), custom_call_target="tpu_custom_call" | custom-call | tf_op jit(solution)/shard_map/pallas_call | solution.py:320
  69.9 1.6 %copy.7 = bf16[128,512]{1,0:T(8,128)(2,1)} copy(bf16[128,512]{1,0:T(8,128)(2,1)} %shard_map.55) | data formatting | bytes 262144

commit v4 on v3

--- a/solution.py
+++ b/solution.py
@@ -34,7 +34,7 @@
     qk_ref, val_ref, buckets_ref, counts_ref, w_buf, out_pack, in_pack, rows_buf, prev_buf, att_buf, out_ret, in_ret, tok_buf, pick_buf,
     pair_out, pair_in, chip_out, chip_in,
     load_sem, w_sem, pack_send, pack_recv, next_send, next_recv, ret_send, ret_recv,
-    pair_send, pair_recv, chip_send, chip_recv,
+    pair_send, pair_recv, chip_send, chip_recv, turn,
 ):
     devices = planes * heads
     slots = devices * CAP
@@ -60,12 +60,29 @@
 
     barrier = pltpu.get_barrier_semaphore()
 
-    def greet(k, carry):
-        other = lax.rem(me + k, devices)
-        pl.semaphore_signal(barrier, inc=1, device_id=(other, mp), device_id_type=MESH)
+    def wrap(i, n):
+        return i - jnp.where(i >= n, n, 0)
+
+    ys = [wrap(y + dy, heads) for dy in range(heads)]
+
+    def group_of(pz):
+        return jnp.where(core == 0, pz, wrap(planes - pz, planes))
+
+    group = group_of(z)
+
+    def plane(a):
+        half = planes // 2
+        return wrap(z + jnp.where(a % 2 == 1, half - (a + 1) // 2, half + a // 2), planes)
+
+    def greet(a, carry):
+        pz = plane(a)
+        for py in ys:
+            pl.semaphore_signal(barrier, inc=1, device_id=(pz * heads + py, mp), device_id_type=MESH)
         return carry
 
-    lax.fori_loop(1, devices, greet, 0)
+    lax.fori_loop(0, planes - 1, greet, 0)
+    for py in ys[1:]:
+        pl.semaphore_signal(barrier, inc=1, device_id=(z * heads + py, mp), device_id_type=MESH)
     pl.semaphore_signal(barrier, inc=1, device_id=(me, x * 2 + 1 - core), device_id_type=MESH)
     for off in range(1, chips):
         there = lax.rem(x + off, chips) * 2 + core
@@ -91,40 +108,48 @@
 
     pl.semaphore_wait(barrier, devices - 1 + chips)
 
-    def peer(i):
-        a = i // heads
-        half = planes // 2
-        dz = jnp.where(lax.rem(a, 2) == 1, half - (a + 1) // 2, half + a // 2)
-        pz = lax.rem(z + dz, planes)
-        py = lax.rem(y + heads - 1 - lax.rem(i, heads), heads)
-        return pz, py
-
-    def pack_copy(p, i):
-        pz, py = peer(i)
-        src = pl.multiple_of(py * slots + pz * unit, unit)
-        dst = pl.multiple_of(me * unit, unit)
-        return pltpu.make_async_remote_copy(
+    def send_pack(p, pz, py):
+        src = pl.multiple_of(py * slots + group_of(pz) * unit, unit)
+        pltpu.make_async_remote_copy(
             src_ref=out_pack.at[p, pl.ds(src, unit)],
-            dst_ref=in_pack.at[p, pl.ds(dst, unit)],
+            dst_ref=in_pack.at[p, pl.ds(own_dst, unit)],
             send_sem=pack_send.at[p],
             recv_sem=pack_recv.at[p, me // 16],
             device_id=(pz * heads + py, mp),
             device_id_type=MESH,
-        )
-
-    own_src = pl.multiple_of(y * slots + z * unit, unit)
+        ).start()
+
+    own_src = pl.multiple_of(y * slots + group * unit, unit)
     own_dst = pl.multiple_of(me * unit, unit)
+    @pl.when(core != 0)
+    def _():
+        pl.semaphore_wait(turn, 1)
+
     for p in range(2):
-        def send_pack(i, carry, p=p):
-            pack_copy(p, i).start()
+        def to_plane(a, carry, p=p):
+            pz = plane(a)
+            for py in ys:
+                send_pack(p, pz, py)
             return carry
 
-        lax.fori_loop(0, devices - 1, send_pack, 0)
+        lax.fori_loop(0, planes - 1, to_plane, 0)
+        for py in ys[1:]:
+            send_pack(p, z, py)
         pltpu.make_async_copy(
             out_pack.at[p, pl.ds(own_src, unit)],
             in_pack.at[p, pl.ds(own_dst, unit)],
             pack_recv.at[p, me // 16],
         ).start()
+
+    most = (devices - 1) * unit
+
+    def wait_sent(p):
+        pltpu.make_async_copy(out_pack.at[p, :most], out_pack.at[p, :most], pack_send.at[p]).wait()
+
+    @pl.when(core == 0)
+    def _():
+        wait_sent(0)
+        pl.semaphore_signal(turn, inc=1, device_id=(me, x * 2 + 1 - core), device_id_type=MESH)
 
     after = iota((tok, tok), 0) > iota((tok, tok), 1)
     for h in range(heads):
@@ -138,7 +163,7 @@
     rank = lax.rem(iota((1, slots), 1), CAP)
     dead = []
     for j in range(-1, heads):
-        b = lax.rem(z * heads + j + devices, devices)
+        b = lax.rem(group * heads + j + devices, devices)
         column = jnp.sum(jnp.where(iota(counts.shape, 1) == b, counts, 0), axis=1, keepdims=True)
         row = jnp.sum(jnp.where(spread, column, 0), axis=0, keepdims=True)
         dead.append(jnp.where(rank < row, 0.0, DEAD))
@@ -163,7 +188,7 @@
                 rows_buf[j, n // 2, g * part : (g + 1) * part, :] = arranged[n * part : (n + 1) * part]
 
     receive(0)
-    next_z = lax.rem(z + 1, planes)
+    next_z = wrap(z + jnp.where(core == 0, 1, planes - 1), planes)
     to_next = pltpu.make_async_remote_copy(
         src_ref=rows_buf.at[heads - 1],
         dst_ref=prev_buf,
@@ -196,34 +221,51 @@
     receive(1)
     to_next.wait_recv()
 
-    def send_ret(c):
-        def body(i, carry):
-            pz, py = peer(i)
-            there = pz * heads + py
-
-            @pl.when(pz // (planes // 2) == c)
+    def send_ret(c, pz, py):
+        there = pz * heads + py
+        pltpu.make_async_remote_copy(
+            src_ref=out_ret.at[pl.ds(pl.multiple_of(there * unit, unit), unit)],
+            dst_ref=in_ret.at[pl.ds(own_src, unit)],
+            send_sem=ret_send.at[c],
+            recv_sem=ret_recv.at[y],
+            device_id=(there, mp),
+            device_id_type=MESH,
+        ).start()
+
+    def send_half(c):
+        def to_plane(a, carry):
+            pz = plane(a)
+
+            @pl.when((pz < 4) == (c == 0))
             def _():
-                pltpu.make_async_remote_copy(
-                    src_ref=out_ret.at[pl.ds(pl.multiple_of(there * unit, unit), unit)],
-                    dst_ref=in_ret.at[pl.ds(own_src, unit)],
-                    send_sem=ret_send,
-                    recv_sem=ret_recv.at[y],
-                    device_id=(there, mp),
-                    device_id_type=MESH,
-                ).start()
+                for py in ys:
+                    send_ret(c, pz, py)
 
             return carry
 
-        lax.fori_loop(0, devices - 1, body, 0)
-
-    for c in range(2):
+        lax.fori_loop(0, planes - 1, to_plane, 0)
+
+    for c, (lo, hi) in enumerate(((0, 1), (1, 4))):
         for j in range(heads - 1):
-            attend(j, rows_buf.at[j - 1] if j else prev_buf, c * slots // 2, slots // 2)
-        for g in range(c * groups // 2, (c + 1) * groups // 2):
+            attend(j, rows_buf.at[j - 1] if j else prev_buf, lo * part, (hi - lo) * part)
+        for g in range(lo, hi):
             rows = slice(g * part, (g + 1) * part)
             mine = jnp.concatenate([att_buf[j, rows, :] for j in range(heads)], axis=0)
             out_ret[g * span : (g + 1) * span, :] = dot(order_back, mine).astype(BF16)
-        send_ret(c)
+        send_half(c)
+        @pl.when((z < 4) == (c == 0))
+        def _():
+            for py in ys[1:]:
+                send_ret(c, z, py)
+        if c == 0 and False:
+            @pl.when(z < 4)
+            def _():
+                here = out_ret.at[: (4 * heads - 1) * unit]
+                pltpu.make_async_copy(here, here, ret_send.at[0]).wait()
+            @pl.when(z >= 4)
+            def _():
+                here = out_ret.at[: 4 * heads * unit]
+                pltpu.make_async_copy(here, here, ret_send.at[0]).wait()
     pltpu.make_async_copy(
         out_ret.at[pl.ds(own_dst, unit)], in_ret.at[pl.ds(own_src, unit)], ret_recv.at[y]
     ).start()
@@ -238,19 +280,7 @@
         return dot(tok_buf[...], w_buf[:, pl.ds(pl.multiple_of(m * block, block), block)])
 
     ways = (2, 1, 3, 0)
-    half = tok // 2
-
-    def to_chip(k, src, way):
-        cx = lax.rem(x + way, chips)
-        copy = pltpu.make_async_remote_copy(
-            src_ref=src,
-            dst_ref=chip_in.at[k],
-            send_sem=chip_send,
-            recv_sem=chip_recv.at[k],
-            device_id=(me, cx * 2 + core),
-            device_id_type=MESH,
-        )
-        copy.start()
+    quarter = tok // 4
 
     def give(k):
         cx = lax.rem(x + ways[k], chips)
@@ -270,38 +300,70 @@
         pltpu.make_async_copy(pair_in.at[k], pair_in.at[k], pair_recv.at[k]).wait()
         return mine + pair_in[k].astype(F32)
 
-    def arrived(k):
-        pltpu.make_async_copy(chip_in.at[k], chip_in.at[k], chip_recv.at[k]).wait()
-        return chip_in[k].astype(F32)
-
-    def put(k, rows, way):
-        chip_out[k] = rows.astype(BF16)
-        to_chip(k, chip_out.at[k], way)
+    def put(first, rows, way):
+        count = rows.shape[0] // quarter
+        here = slice(first, first + count)
+        chip_out[here] = rows.astype(BF16).reshape(count, quarter, block)
+        pltpu.make_async_remote_copy(
+            src_ref=chip_out.at[here],
+            dst_ref=chip_in.at[here],
+            send_sem=chip_send,
+            recv_sem=chip_recv.at[first],
+            device_id=(me, lax.rem(x + way, chips) * 2 + core),
+            device_id_type=MESH,
+        ).start()
+
+    def wait_chip(first, count):
+        here = chip_in.at[first : first + count]
+        pltpu.make_async_copy(here, here, chip_recv.at[first]).wait()
+
+    def part_of(rows, q):
+        return rows[q * quarter : (q + 1) * quarter]
 
     give(0)
     give(1)
     opposite = pair_sum(0)
-    put(0, opposite[:half], 1)
-    put(1, opposite[half:], 3)
+    for q in (0, 2, 1, 3):
+        put(q, part_of(opposite, q), 1 if q < 2 else 3)
     give(2)
     right = pair_sum(1)
-    put(2, right[half:], 1)
+    put(4, right[2 * quarter :], 1)
     give(3)
     left = pair_sum(2)
-    put(3, left[:half], 3)
-    put(4, right[:half] + arrived(0), 1)
-    put(5, left[half:] + arrived(1), 3)
+    put(6, left[: 2 * quarter], 3)
+    for q in (0, 2, 1, 3):
+        wait_chip(q, 1)
+        put(8 + q, part_of(right if q < 2 else left, q) + chip_in[q].astype(F32), 1 if q < 2 else 3)
     total = pair_sum(3)
-    upper = total[:half] + arrived(3)
-    lower = total[half:] + arrived(2)
-    out_ref[:half, :] = (upper + arrived(4)).astype(BF16)
-    out_ref[half:, :] = (lower + arrived(5)).astype(BF16)
-
-    most = (devices - 1) * unit
-    for p in range(2):
-        pltpu.make_async_copy(out_pack.at[p, :most], out_pack.at[p, :most], pack_send.at[p]).wait()
+    wait_chip(4, 2)
+    wait_chip(6, 2)
+    for q in (0, 2, 1, 3):
+        near = part_of(total, q) + chip_in[(6, 7, 4, 5)[q]].astype(F32)
+        wait_chip(8 + q, 1)
+        out_ref[q * quarter : (q + 1) * quarter, :] = (near + chip_in[8 + q].astype(F32)).astype(BF16)
+
+    @pl.when(core != 0)
+    def _():
+        wait_sent(0)
+
+    wait_sent(1)
     to_next.wait_send()
-    pltpu.make_async_copy(out_ret.at[:most], out_ret.at[:most], ret_send).wait()
+    @pl.when(z < 4)
+    def _():
+        here = out_ret.at[: (4 * heads - 1) * unit]
+        pltpu.make_async_copy(here, here, ret_send.at[0]).wait()
+    @pl.when(z >= 4)
+    def _():
+        here = out_ret.at[: 4 * heads * unit]
+        pltpu.make_async_copy(here, here, ret_send.at[0]).wait()
+    @pl.when(z >= 4)
+    def _():
+        here = out_ret.at[: (12 * heads - 1) * unit]
+        pltpu.make_async_copy(here, here, ret_send.at[1]).wait()
+    @pl.when(z < 4)
+    def _():
+        here = out_ret.at[: 12 * heads * unit]
+        pltpu.make_async_copy(here, here, ret_send.at[1]).wait()
     pltpu.make_async_copy(pair_out, pair_out, pair_send).wait()
     pltpu.make_async_copy(chip_out, chip_out, chip_send).wait()
 
@@ -339,20 +401,21 @@
             pltpu.VMEM((heads, tok, slots), BF16),
             pltpu.VMEM((chips, tok, block), BF16),
             pltpu.VMEM((chips, tok, block), BF16),
-            pltpu.VMEM((6, tok // 2, block), BF16),
-            pltpu.VMEM((6, tok // 2, block), BF16),
+            pltpu.VMEM((12, tok // 4, block), BF16),
+            pltpu.VMEM((12, tok // 4, block), BF16),
             dma((4,)),
             dma,
             dma((2,)),
             dma((2, groups)),
             dma,
             dma,
-            dma,
+            dma((2,)),
             dma((heads,)),
             dma,
             dma((chips,)),
             dma,
-            dma((6,)),
+            dma((12,)),
+            pltpu.SemaphoreType.REGULAR,
         ],
         compiler_params=pltpu.CompilerParams(
             collective_id=0, has_side_effects=True, vmem_limit_bytes=60 * 1024 * 1024

time: 71.6 us -> 69.5 us (0.971)
  the two profiles are of different devices: /device:TPU:1 before, /device:TPU:128 now
where the time goes in v4:
time: 69.5 us; the launch traced here: 69.4 us
  Pallas kernels  67.8 us (98%)
  local copies, waits for them, and re-layouts  1.57 us (2%)
    pallas_call x1, Pallas kernels, local(): pl.pallas_call(functools.partial(layer_kernel, planes, heads, chips, tok,...  67.8 us
    unnamed x1, local copies, waits for them, and re-layouts  1.57 us

profile of v4, /device:TPU:128, one launch (start us, length us, event | category | flops | bytes accessed | tf_op | source)
XLA Modules:
  0.0 69.4 jit_solution(835174450360132685)
XLA Ops:
  0.0 67.8 %shard_map.55 = bf16[128,512]{1,0:T(8,128)(2,1)} custom-call(bf16[128,512]{1,0:T(8,128)(2,1)} %qk_hbm.1, bf16[128,512]{1,0:T(8,128)(2,1)} %val_hbm.1, s32[4,128]{1,0:T(4,128)} %bitcast.1, s32[64,4,64]{2,1,0:T(4,128)} %counts_hbm.1, bf16[512,4096]{1,0:T(8,128)(2,1)} %w_hbm.1), custom_call_target="tpu_custom_call" | custom-call | tf_op jit(solution)/shard_map/pallas_call | solution.py:382
  67.8 1.6 %copy.7 = bf16[128,512]{1,0:T(8,128)(2,1)} copy(bf16[128,512]{1,0:T(8,128)(2,1)} %shard_map.55) | data formatting | bytes 262144

commit v5 on v4

--- a/solution.py
+++ b/solution.py
@@ -11,6 +11,7 @@
 CAP = 4
 SELF_SCORE = -100000.0
 DEAD = -1e30
+LOG2E = math.log2(math.e)
 BF16 = jnp.bfloat16
 F32 = jnp.float32
 MESH = pl.DeviceIdType.MESH
@@ -121,11 +122,12 @@
 
     own_src = pl.multiple_of(y * slots + group * unit, unit)
     own_dst = pl.multiple_of(me * unit, unit)
-    @pl.when(core != 0)
-    def _():
-        pl.semaphore_wait(turn, 1)
-
     for p in range(2):
+        if p == 1:
+            @pl.when(core != 0)
+            def _():
+                pl.semaphore_wait(turn, 1)
+
         def to_plane(a, carry, p=p):
             pz = plane(a)
             for py in ys:
@@ -148,7 +150,7 @@
 
     @pl.when(core == 0)
     def _():
-        wait_sent(0)
+        wait_sent(1)
         pl.semaphore_signal(turn, inc=1, device_id=(me, x * 2 + 1 - core), device_id_type=MESH)
 
     after = iota((tok, tok), 0) > iota((tok, tok), 1)
@@ -206,20 +208,18 @@
         rows = slice(first, first + count)
         itself = iota((count, slots), 0) + first == iota((count, slots), 1)
         q = rows_buf[j, 0, rows, :]
-        own = lax.dot_general(q, rows_buf[j, 0], trans, preferred_element_type=F32)
-        own = jnp.where(itself, SELF_SCORE, own * scale + dead[j + 1])
-        far = lax.dot_general(q, prev[0], trans, preferred_element_type=F32) * scale + dead[j]
+        own = lax.dot_general(q, rows_buf[j, 0], trans, preferred_element_type=F32) + dead[j + 1]
+        own = jnp.where(itself, SELF_SCORE / scale, own)
+        far = lax.dot_general(q, prev[0], trans, preferred_element_type=F32) + dead[j]
         top = jnp.maximum(jnp.max(own, axis=1, keepdims=True), jnp.max(far, axis=1, keepdims=True))
-        own = jnp.exp(own - top)
-        far = jnp.exp(far - top)
-        total = jnp.sum(own, axis=1, keepdims=True) + jnp.sum(far, axis=1, keepdims=True)
-        share = 1.0 / total
+        own = jnp.exp2((own - top) * (scale * LOG2E))
+        far = jnp.exp2((far - top) * (scale * LOG2E))
+        share = 1.0 / (jnp.sum(own, axis=1, keepdims=True) + jnp.sum(far, axis=1, keepdims=True))
         att = dot((own * share).astype(BF16), rows_buf[j, 1]) + dot((far * share).astype(BF16), prev[1])
         att_buf[j, rows, :] = att.astype(BF16)
 
     attend(heads - 1, rows_buf.at[heads - 2], 0, slots)
     receive(1)
-    to_next.wait_recv()
 
     def send_ret(c, pz, py):
         there = pz * heads + py
@@ -232,40 +232,47 @@
             device_id_type=MESH,
         ).start()
 
-    def send_half(c):
+    def send_rest():
         def to_plane(a, carry):
             pz = plane(a)
 
-            @pl.when((pz < 4) == (c == 0))
+            @pl.when(pz >= 8)
             def _():
                 for py in ys:
-                    send_ret(c, pz, py)
+                    send_ret(1, pz, py)
 
             return carry
 
         lax.fori_loop(0, planes - 1, to_plane, 0)
 
     for c, (lo, hi) in enumerate(((0, 1), (1, 4))):
-        for j in range(heads - 1):
+        for j in (*range(1, heads - 1), 0):
+            if j == 0 and c == 0:
+                to_next.wait_recv()
             attend(j, rows_buf.at[j - 1] if j else prev_buf, lo * part, (hi - lo) * part)
         for g in range(lo, hi):
             rows = slice(g * part, (g + 1) * part)
             mine = jnp.concatenate([att_buf[j, rows, :] for j in range(heads)], axis=0)
             out_ret[g * span : (g + 1) * span, :] = dot(order_back, mine).astype(BF16)
-        send_half(c)
+        if c == 0:
+            for pz in range(4):
+                @pl.when(z != pz)
+                def _(pz=pz):
+                    for py in ys:
+                        send_ret(c, pz, py)
+        else:
+            for pz in range(4, 8):
+                @pl.when(z != pz)
+                def _(pz=pz):
+                    for py in ys:
+                        send_ret(c, pz, py)
+            send_rest()
+
         @pl.when((z < 4) == (c == 0))
         def _():
             for py in ys[1:]:
                 send_ret(c, z, py)
-        if c == 0 and False:
-            @pl.when(z < 4)
-            def _():
-                here = out_ret.at[: (4 * heads - 1) * unit]
-                pltpu.make_async_copy(here, here, ret_send.at[0]).wait()
-            @pl.when(z >= 4)
-            def _():
-                here = out_ret.at[: 4 * heads * unit]
-                pltpu.make_async_copy(here, here, ret_send.at[0]).wait()
+
     pltpu.make_async_copy(
         out_ret.at[pl.ds(own_dst, unit)], in_ret.at[pl.ds(own_src, unit)], ret_recv.at[y]
     ).start()
@@ -344,9 +351,9 @@
 
     @pl.when(core != 0)
     def _():
-        wait_sent(0)
-
-    wait_sent(1)
+        wait_sent(1)
+
+    wait_sent(0)
     to_next.wait_send()
     @pl.when(z < 4)
     def _():

time: 69.5 us -> 67.4 us (0.970)
  the two profiles are of different devices: /device:TPU:128 before, /device:TPU:64 now
where the time goes in v5:
time: 67.4 us; the launch traced here: 67.3 us
  Pallas kernels  65.7 us (97%)
  local copies, waits for them, and re-layouts  1.57 us (2%)
    pallas_call x1, Pallas kernels, local(): pl.pallas_call(functools.partial(layer_kernel, planes, heads, chips, tok,...  65.7 us
    unnamed x1, local copies, waits for them, and re-layouts  1.57 us

profile of v5, /device:TPU:64, one launch (start us, length us, event | category | flops | bytes accessed | tf_op | source)
XLA Modules:
  0.0 67.3 jit_solution(3110146166157178392)
XLA Ops:
  0.0 65.7 %shard_map.55 = bf16[128,512]{1,0:T(8,128)(2,1)} custom-call(bf16[128,512]{1,0:T(8,128)(2,1)} %qk_hbm.1, bf16[128,512]{1,0:T(8,128)(2,1)} %val_hbm.1, s32[4,128]{1,0:T(4,128)} %bitcast.1, s32[64,4,64]{2,1,0:T(4,128)} %counts_hbm.1, bf16[512,4096]{1,0:T(8,128)(2,1)} %w_hbm.1), custom_call_target="tpu_custom_call" | custom-call | tf_op jit(solution)/shard_map/pallas_call | solution.py:389
  65.7 1.6 %copy.7 = bf16[128,512]{1,0:T(8,128)(2,1)} copy(bf16[128,512]{1,0:T(8,128)(2,1)} %shard_map.55) | data formatting | bytes 262144

commit v6 on v5

--- a/solution.py
+++ b/solution.py
@@ -245,7 +245,7 @@
 
         lax.fori_loop(0, planes - 1, to_plane, 0)
 
-    for c, (lo, hi) in enumerate(((0, 1), (1, 4))):
+    for c, (lo, hi) in enumerate(((0, 1), (1, 2), (2, 4))):
         for j in (*range(1, heads - 1), 0):
             if j == 0 and c == 0:
                 to_next.wait_recv()
@@ -254,24 +254,20 @@
             rows = slice(g * part, (g + 1) * part)
             mine = jnp.concatenate([att_buf[j, rows, :] for j in range(heads)], axis=0)
             out_ret[g * span : (g + 1) * span, :] = dot(order_back, mine).astype(BF16)
-        if c == 0:
-            for pz in range(4):
+        sem = min(c, 1)
+        if c < 2:
+            for pz in range(4 * lo, 4 * hi):
                 @pl.when(z != pz)
                 def _(pz=pz):
                     for py in ys:
-                        send_ret(c, pz, py)
+                        send_ret(sem, pz, py)
         else:
-            for pz in range(4, 8):
-                @pl.when(z != pz)
-                def _(pz=pz):
-                    for py in ys:
-                        send_ret(c, pz, py)
             send_rest()
 
-        @pl.when((z < 4) == (c == 0))
+        @pl.when((z >= 4 * lo) & (z < 4 * hi))
         def _():
             for py in ys[1:]:
-                send_ret(c, z, py)
+                send_ret(sem, z, py)
 
     pltpu.make_async_copy(
         out_ret.at[pl.ds(own_dst, unit)], in_ret.at[pl.ds(own_src, unit)], ret_recv.at[y]

time: 67.4 us -> 67.4 us (level)
  the two profiles are of different devices: /device:TPU:64 before, /device:TPU:160 now
where the time goes in v6:
time: 67.4 us; the launch traced here: 67.3 us
  Pallas kernels  65.7 us (97%)
  local copies, waits for them, and re-layouts  1.57 us (2%)
    pallas_call x1, Pallas kernels, local(): pl.pallas_call(functools.partial(layer_kernel, planes, heads, chips, tok,...  65.7 us
    unnamed x1, local copies, waits for them, and re-layouts  1.57 us

profile of v6, /device:TPU:160, one launch (start us, length us, event | category | flops | bytes accessed | tf_op | source)
XLA Modules:
  0.0 67.3 jit_solution(8268161327592236466)
XLA Ops:
  0.0 65.7 %shard_map.55 = bf16[128,512]{1,0:T(8,128)(2,1)} custom-call(bf16[128,512]{1,0:T(8,128)(2,1)} %qk_hbm.1, bf16[128,512]{1,0:T(8,128)(2,1)} %val_hbm.1, s32[4,128]{1,0:T(4,128)} %bitcast.1, s32[64,4,64]{2,1,0:T(4,128)} %counts_hbm.1, bf16[512,4096]{1,0:T(8,128)(2,1)} %w_hbm.1), custom_call_target="tpu_custom_call" | custom-call | tf_op jit(solution)/shard_map/pallas_call | solution.py:385
  65.7 1.6 %copy.7 = bf16[128,512]{1,0:T(8,128)(2,1)} copy(bf16[128,512]{1,0:T(8,128)(2,1)} %shard_map.55) | data formatting | bytes 262144
